TPU v7x, 32 devices: a whole 2x2x4 slice. The times are simulated.
32 devices in a mesh: seq: 8 (over z, x), head: 4 (over y, core).
Axes of the slice: x: 2, y: 2, z: 4, core: 2. Of those that a mesh axis runs over, the one named last changes fastest.
Arguments:
- qkv_pre: bfloat16 [4096, 3, 16, 128], P(('seq', 'head')), may hold values from -10 to 10
- grad_out: bfloat16 [4096, 2048], P(('seq', 'head')), may hold values from -48 to 48
- out_values: bfloat16 [2048, 2048], P('head'), may hold values from -4 to 4
- out_scales: float32 [16, 16], replicated, may hold values from 0.01 to 0.04
- conv_kernel: float32 [31, 3, 16, 128], P(None, None, 'head'), may hold values from -1 to 1
- window: int32 [16], replicated, may hold values from 64 to 96, as said below
- offsets: int32 [8], replicated, may hold values from 0 to 32, as said below
Outputs:
- grad_pre: bfloat16 [4096, 3, 16, 128], P(('seq', 'head'))
Inputs may be any that keep to these rules, and one draw needn't show every extreme that they name: window[h] + offsets[b] <= 128 for every head h and block b; some head has window exactly 96. offsets[b] <= 32 for every block b, with equality in at least one block.
All inputs are finite; a program needn't handle non-finite values.
Results may differ from a plain program's by a relative error of at most 0.005.
The roundings to bfloat16 on the way count: a program that leaves them out, or rounds other values in their place, can miss the bound.
Values may be sent and summed in bfloat16 or wider, within the bound.
No kernel may reach another device: no remote copies, remote signals or barrier semaphores. Data moves between devices by JAX's collectives and lax.ppermute only.
A program may use at most 64 MiB of HBM per device.

v0:
```python
import math
import jax
import jax.numpy as jnp
from jax import lax
from jax.sharding import PartitionSpec as P

KW = 31
MASKB = 512


def shifted(value, axis, by):
    length = lax.axis_size(axis)
    pairs = [(i, i + by) for i in range(length) if 0 <= i + by < length]
    return lax.ppermute(value, axis, pairs)


def causal_conv(series, kernel):
    length = series.shape[0]
    padded = jnp.concatenate(
        [jnp.zeros((KW - 1,) + series.shape[1:], series.dtype), series], axis=0
    )
    summed = jnp.zeros(series.shape, jnp.float32)
    for kernel_tap in range(KW):
        first_row = KW - 1 - kernel_tap
        summed = summed + kernel[kernel_tap] * padded[first_row : first_row + length].astype(
            jnp.float32
        )
    return summed


def transposed_conv(grads, kernel):
    length = grads.shape[0]
    padded = jnp.concatenate([grads, jnp.zeros((KW - 1,) + grads.shape[1:], jnp.float32)], axis=0)
    summed = jnp.zeros(grads.shape, jnp.float32)
    for kernel_tap in range(KW):
        summed = summed + kernel[kernel_tap] * padded[kernel_tap : kernel_tap + length]
    return summed


def dequantize(values, start, out_scales):
    row_count = values.shape[0]
    full_width = values.shape[1]
    block_count = out_scales.shape[0]
    block_size = full_width // out_scales.shape[1]
    column_scales = jnp.repeat(out_scales, block_size, axis=1)
    row_block = (start + lax.iota(jnp.int32, row_count)) // block_size
    picker = (row_block[:, None] == lax.iota(jnp.int32, block_count)[None, :]).astype(jnp.float32)
    scales = jnp.dot(picker, column_scales, precision=lax.Precision.HIGHEST)
    return (values.astype(jnp.float32) * scales).astype(jnp.bfloat16)


def per_device(qkv_pre, grad_out, out_values, out_scales, conv_kernel, window, offsets):
    tok_rows = qkv_pre.shape[0]
    head_count = qkv_pre.shape[2]
    head_dim = qkv_pre.shape[3]
    n_head = lax.axis_size("head")
    local_heads = head_count // n_head
    seq_rows = tok_rows * n_head
    span = seq_rows // 4
    margin = MASKB // 4
    prior = span + margin
    ext_rows = prior + seq_rows
    seq_index = lax.axis_index("seq")
    head_index = lax.axis_index("head")
    inv_scale = 1.0 / math.sqrt(head_dim)
    local_window = lax.dynamic_slice_in_dim(window, head_index * local_heads, local_heads, 0)
    weight = dequantize(out_values, head_index * out_values.shape[0], out_scales)
    grad_heads = lax.dot_general(
        lax.all_gather(grad_out, "head", axis=0, tiled=True),
        weight,
        (((1,), (1,)), ((), ())),
        preferred_element_type=jnp.float32,
    ).astype(jnp.bfloat16)
    grad_heads = grad_heads.reshape(seq_rows, local_heads, head_dim)
    mixed_in = lax.all_to_all(qkv_pre, "head", split_axis=2, concat_axis=0, tiled=True)
    tail_rows = mixed_in[seq_rows - prior :]
    before = shifted(tail_rows, "seq", 1)
    extended = jnp.concatenate([before, mixed_in], axis=0)
    mixed_rows = causal_conv(extended, conv_kernel).astype(jnp.bfloat16)
    query_rows = mixed_rows[prior:, 0]
    key_rows = mixed_rows[:, 1]
    value_rows = mixed_rows[:, 2]
    n_blocks = seq_rows // MASKB
    key_len = span + MASKB
    reach_base = seq_index * n_blocks

    def attend(block_index, totals):
        grad_q, grad_k, grad_v = totals
        q_start = block_index * MASKB
        k_start = margin + q_start
        q_block = lax.dynamic_slice_in_dim(query_rows, q_start, MASKB, 0)
        o_block = lax.dynamic_slice_in_dim(grad_heads, q_start, MASKB, 0)
        k_block = lax.dynamic_slice_in_dim(key_rows, k_start, key_len, 0)
        v_block = lax.dynamic_slice_in_dim(value_rows, k_start, key_len, 0)
        scores = (
            jnp.einsum("qhe,khe->hqk", q_block, k_block, preferred_element_type=jnp.float32)
            * inv_scale
        )
        query_pos = seq_index * seq_rows + q_start + lax.iota(jnp.int32, MASKB)
        key_pos = seq_index * seq_rows - prior + k_start + lax.iota(jnp.int32, key_len)
        distance = query_pos[:, None] - key_pos[None, :]
        reach_now = local_window + lax.dynamic_index_in_dim(
            offsets, reach_base + block_index, 0, keepdims=False
        )
        allowed = ((distance >= 0) & (key_pos[None, :] >= 0))[None] & (
            distance[None] <= reach_now[:, None, None]
        )
        row_top = jnp.max(jnp.where(allowed, scores, -1e30), axis=2, keepdims=True)
        exp_scores = jnp.where(allowed, jnp.exp(scores - row_top), 0.0)
        probs = exp_scores / jnp.sum(exp_scores, axis=2, keepdims=True)
        probs_b = probs.astype(jnp.bfloat16)
        d_prob = jnp.einsum("qhe,khe->hqk", o_block, v_block, preferred_element_type=jnp.float32)
        row_delta = jnp.sum(probs * d_prob, axis=2, keepdims=True)
        d_score = (probs * (d_prob - row_delta) * inv_scale).astype(jnp.bfloat16)
        grad_q_block = jnp.einsum(
            "hqk,khe->qhe", d_score, k_block, preferred_element_type=jnp.float32
        )
        grad_k_block = jnp.einsum(
            "hqk,qhe->khe", d_score, q_block, preferred_element_type=jnp.float32
        )
        grad_v_block = jnp.einsum(
            "hqk,qhe->khe", probs_b, o_block, preferred_element_type=jnp.float32
        )
        grad_q = lax.dynamic_update_slice_in_dim(grad_q, grad_q_block, q_start, 0)
        grad_k = lax.dynamic_update_slice_in_dim(
            grad_k, lax.dynamic_slice_in_dim(grad_k, k_start, key_len, 0) + grad_k_block, k_start, 0
        )
        grad_v = lax.dynamic_update_slice_in_dim(
            grad_v, lax.dynamic_slice_in_dim(grad_v, k_start, key_len, 0) + grad_v_block, k_start, 0
        )
        return (grad_q, grad_k, grad_v)

    start_totals = (
        jnp.zeros((seq_rows, local_heads, head_dim), jnp.float32),
        jnp.zeros((ext_rows, local_heads, head_dim), jnp.float32),
        jnp.zeros((ext_rows, local_heads, head_dim), jnp.float32),
    )
    grad_q, grad_k, grad_v = lax.fori_loop(0, n_blocks, attend, start_totals)
    grad_q_ext = jnp.concatenate(
        [jnp.zeros((prior, local_heads, head_dim), jnp.float32), grad_q], axis=0
    )
    grads = jnp.stack([grad_q_ext, grad_k, grad_v], axis=1)
    spread = transposed_conv(grads, conv_kernel)
    returned = shifted(spread[:prior].astype(jnp.bfloat16), "seq", -1)
    own_rows = spread[prior:]
    tail_sum = own_rows[seq_rows - prior :] + returned.astype(jnp.float32)
    result = jnp.concatenate([own_rows[: seq_rows - prior], tail_sum], axis=0).astype(jnp.bfloat16)
    return lax.all_to_all(result, "head", split_axis=0, concat_axis=2, tiled=True)


def solution(mesh):
    return jax.shard_map(
        per_device,
        mesh=mesh,
        in_specs=(
            P(("seq", "head"), None, None, None),
            P(("seq", "head"), None),
            P("head", None),
            P(),
            P(None, None, "head", None),
            P(),
            P(),
        ),
        out_specs=P(("seq", "head"), None, None, None),
        check_vma=False,
    )
```

profile of v0, /device:TPU:0, one launch (start us, length us, event | category | flops | bytes accessed | tf_op | source)
XLA Modules:
  0.0 214.1 jit_solution(17763769929687273269)
XLA Ops:
  6.5 3.0 %copy.26 = bf16[128,3,16,128]{3,0,1,2:T(8,128)(2,1)} copy(bf16[128,3,16,128]{3,2,1,0:T(8,128)(2,1)} %param.7) | data formatting | bytes 3145728 | tf_op args[0]
  9.5 4.4 %all-to-all-start = ((bf16[128,3,16,128]{3,0,1,2:T(8,128)(2,1)}), bf16[128,3,16,128]{3,0,1,2:T(8,128)(2,1)S(1)}, u32[]{:S(2)}, u32[]{:S(2)}) async-start(bf16[128,3,16,128]{3,0,1,2:T(8,128)(2,1)} %copy.26), calls=%async_computation | async-start | bytes 3145728 | tf_op jit(solution)/shard_map/all_to_all | solution.py:75
  13.9 0.7 all-gather.2.cloned.1.call-update
  14.7 0.7 dynamic_slice.31
  15.3 0.7 dynamic-slice_add_fusion
  16.3 1.1 compare_and_fusion.2
  17.4 22.6 %all-to-all-done = bf16[128,3,16,128]{3,0,1,2:T(8,128)(2,1)S(1)} async-done(((bf16[128,3,16,128]{3,0,1,2:T(8,128)(2,1)}), bf16[128,3,16,128]{3,0,1,2:T(8,128)(2,1)S(1)}, u32[]{:S(2)}, u32[]{:S(2)}) %all-to-all-start) | async-done | bytes 1572896 | tf_op jit(solution)/shard_map/all_to_all | solution.py:75
  40.0 0.2 copy.49
  40.2 4.9 %collective-permute-start = (bf16[256,3,4,128]{3,0,2,1:T(8,128)(2,1)S(1)}, bf16[256,3,4,128]{3,0,2,1:T(8,128)(2,1)S(1)}, u32[]{:S(2)}, u32[]{:S(2)}) collective-permute-start(bf16[256,3,4,128]{3,0,2,1:T(8,128)(2,1)S(1)} %bitcast.129), channel_id=1, source_target_pairs={{0,4},{4,8},{8,12},{12,16},{16,20},{20,24},{24,28},{1,5},{5,9},{9,... | collective-permute-start | bytes 2359304 | tf_op jit(solution)/shard_map/ppermute | solution.py:14
  45.2 1.3 broadcast_subtract_fusion
  46.6 3.3 %multiply_convert_fusion.1 = bf16[512,2048]{1,0:T(8,128)(2,1)} fusion(bf16[512,2048]{1,0:T(8,128)(2,1)S(1)} %copy-done.2, f32[2,8,16,128]{3,2,1,0:T(8,128)S(1)} %bitcast.132, s32[512]{0:T(512)S(1)} %add_select_fusion), kind=kOutput, calls=%fused_computation.16 | convolution fusion | flops 204480512 | bytes 4327424 | tf_op jit(solution)/shard_map/dot_general | solution.py:48
  49.9 11.0 %collective-permute-done = bf16[256,3,4,128]{3,0,2,1:T(8,128)(2,1)S(1)} collective-permute-done((bf16[256,3,4,128]{3,0,2,1:T(8,128)(2,1)S(1)}, bf16[256,3,4,128]{3,0,2,1:T(8,128)(2,1)S(1)}, u32[]{:S(2)}, u32[]{:S(2)}) %collective-permute-start) | collective-permute-done | bytes 786464 | tf_op jit(solution)/shard_map/ppermute | solution.py:14
  60.9 0.9 pad_maximum_fusion.1
  61.9 20.5 %add_convert_fusion = bf16[768,3,4,128]{3,0,2,1:T(8,128)(2,1)} fusion(bf16[798,3,4,128]{3,0,2,1:T(8,128)(2,1)S(1)} %pad_maximum_fusion.1, bf16[512,3,4,128]{3,0,2,1:T(8,128)(2,1)} %bitcast.126, bf16[256,3,4,128]{3,0,2,1:T(8,128)(2,1)S(1)} %collective-permute-done, f32[3,4,128]{2,1,0:T(4,128)S(1)} %get-tuple-element.76, ...), kind=kLoop, calls=%fused_computation.15 | loop fusion | flops 113246208 | bytes 75687936 | tf_op jit(solution)/shard_map/convert_element_type | solution.py:79
  82.4 9.2 %fusion.54 = (f32[4,512]{1,0:T(4,128)}, f32[4,512,640]{2,1,0:T(8,128)}) fusion(s32[512,640]{1,0:T(8,128)} %broadcast_subtract_fusion, s32[4]{0:T(128)S(1)} %dynamic-slice_add_fusion, pred[512,640]{1,0:T(8,128)(4,1)} %compare_and_fusion.2, bf16[768,3,4,128]{3,0,2,1:T(8,128)(2,1)} %add_convert_fusion), kind=kOutput, calls=%fused_computation.105 | convolution fusion | flops 684196480 | bytes 10888192 | tf_op jit(solution)/shard_map/while/body/eval_jaxpr/sub | solution.py:109
  91.6 3.6 %convolution_convert_fusion = bf16[512,512]{1,0:T(8,128)(2,1)S(1)} fusion(bf16[512,2048]{1,0:T(8,128)(2,1)} %multiply_convert_fusion.1, bf16[512,2048]{1,0:T(8,128)(2,1)} %all-gather.2.cloned.1.call-done), kind=kOutput, calls=%fused_computation.40 | convolution fusion | flops 1074003968 | bytes 4718592 | tf_op jit(solution)/shard_map/dot_general | solution.py:68
  95.3 3.3 %fusion.38 = f32[4,512,640]{2,1,0:T(8,128)} fusion(bf16[512,4,128]{0,2,1:T(8,128)(2,1)S(1)} %bitcast.130, bf16[768,3,4,128]{3,0,2,1:T(8,128)(2,1)S(1)} %copy-done.1), kind=kOutput, calls=%fused_computation.43 | convolution fusion | flops 335544320 | bytes 6422528 | tf_op jit(solution)/shard_map/while/body/eval_jaxpr/qhe,khe->hqk/dot_general | solution.py:112
  98.6 17.9 %fusion.33 = f32[512,4,128]{2,0,1:T(8,128)S(1)} fusion(f32[4,512,640]{2,1,0:T(8,128)} %fusion.38, bf16[768,3,4,128]{3,0,2,1:T(8,128)(2,1)S(1)} %copy-done.1, f32[4,512,640]{2,1,0:T(8,128)} %get-tuple-element.79, f32[4,512]{1,0:T(4,128)} %get-tuple-element.78), kind=kOutput, calls=%fused_computation.38 | convolution fusion | flops 344722048 | bytes 22691840 | tf_op jit(solution)/shard_map/while/body/eval_jaxpr/hqk,khe->qhe/dot_general | solution.py:115
  116.5 20.8 %fusion.30 = f32[640,4,128]{2,0,1:T(8,128)} fusion(f32[4,512,640]{2,1,0:T(8,128)} %fusion.38, bf16[768,3,4,128]{3,0,2,1:T(8,128)(2,1)S(1)} %copy-done.1, f32[4,512,640]{2,1,0:T(8,128)} %get-tuple-element.79, f32[4,512]{1,0:T(4,128)} %get-tuple-element.78), kind=kOutput, calls=%fused_computation.37 | convolution fusion | flops 344722048 | bytes 22822912 | tf_op jit(solution)/shard_map/while/body/eval_jaxpr/hqk,qhe->khe/dot_general | solution.py:118
  137.2 4.1 %fusion.27 = f32[640,4,128]{2,0,1:T(8,128)S(1)} fusion(bf16[512,4,128]{0,2,1:T(8,128)(2,1)} %bitcast.131, f32[4,512,640]{2,1,0:T(8,128)} %get-tuple-element.79, f32[4,512]{1,0:T(4,128)} %get-tuple-element.78), kind=kOutput, calls=%fused_computation.36 | convolution fusion | flops 338165760 | bytes 7086080 | tf_op jit(solution)/shard_map/while/body/eval_jaxpr/hqk,qhe->khe/dot_general | solution.py:121
  141.5 0.2 pad_bitcast_fusion
  141.8 0.3 pad_maximum_fusion
  142.2 0.2 copy-done.7
  142.6 18.6 %fusion.52 = (bf16[768,3,4,128]{3,0,2,1:T(8,128)(2,1)S(1)}, f32[768,3,4,128]{3,0,2,1:T(8,128)S(1)}) fusion(f32[3,4,128]{2,1,0:T(4,128)S(1)} %get-tuple-element.76, f32[3,4,128]{2,1,0:T(4,128)S(1)} %get-tuple-element.77, f32[3,4,128]{2,1,0:T(4,128)S(1)} %get-tuple-element.34, f32[3,4,128]{2,1,0:T(4,128)S(1)} %get-tuple-element.35, ...), kind=kLoop, calls=%fused_computation.103 | loop fusion | flops 73138176 | bytes 11986944 | tf_op jit(solution)/shard_map/convert.2
  161.2 0.1 fusion.53
  161.4 1.3 collective-permute-start.1
  162.7 18.7 %collective-permute-done.1 = bf16[256,3,4,128]{3,0,2,1:T(8,128)(2,1)S(1)} collective-permute-done((bf16[256,3,4,128]{3,0,2,1:T(8,128)(2,1)S(1)}, bf16[256,3,4,128]{3,0,2,1:T(8,128)(2,1)S(1)}, u32[]{:S(2)}, u32[]{:S(2)}) %collective-permute-start.1) | collective-permute-done | bytes 786464 | tf_op jit(solution)/shard_map/ppermute | solution.py:14
  181.4 0.2 fusion.26
  181.6 0.1 pad_maximum_fusion.2
  181.7 1.2 copy.34
  182.9 22.7 %all_to_all.36 = bf16[512,3,4,128]{3,2,1,0:T(4,128)(2,1)S(1)} all-to-all(bf16[512,3,4,128]{3,2,1,0:T(4,128)(2,1)S(1)} %copy.34), channel_id=1, replica_groups=mesh['seq'=8,'head'=4] {'head'}, dimensions={0} | all-to-all | bytes 3145728 | tf_op jit(solution)/shard_map/all_to_all | solution.py:148
  205.6 1.7 copy.35
  (82 shorter events, 0.6 us)
Async XLA Ops:
  6.5 8.1 %copy-start.34 = (s32[8]{0:T(128)S(1)}, s32[8]{0:T(128)}, u32[]{:S(2)}) copy-start(s32[8]{0:T(128)} %param.13) | copy-start | bytes 100
  6.5 8.8 %copy-start.33 = (s32[16]{0:T(128)S(1)}, s32[16]{0:T(128)}, u32[]{:S(2)}) copy-start(s32[16]{0:T(128)} %param.12) | copy-start | bytes 196
  6.5 9.6 %copy-start.5 = (f32[31,3,4,128]{3,2,1,0:T(4,128)S(1)}, f32[31,3,4,128]{3,2,1,0:T(4,128)}, u32[]{:S(2)}) copy-start(f32[31,3,4,128]{3,2,1,0:T(4,128)} %param.11) | copy-start | bytes 571396
  9.5 36.9 %copy-start.32 = (f32[16,16]{1,0:T(8,128)S(1)}, f32[16,16]{1,0:T(8,128)}, u32[]{:S(2)}) copy-start(f32[16,16]{1,0:T(8,128)} %param.10) | copy-start | bytes 3076
  9.5 30.4 %all-to-all-start = ((bf16[128,3,16,128]{3,0,1,2:T(8,128)(2,1)}), bf16[128,3,16,128]{3,0,1,2:T(8,128)(2,1)S(1)}, u32[]{:S(2)}, u32[]{:S(2)}) async-start(bf16[128,3,16,128]{3,0,1,2:T(8,128)(2,1)} %copy.26), calls=%async_computation | async-start | bytes 3145728 | tf_op jit(solution)/shard_map/all_to_all | solution.py:75
  13.9 77.7 %all-gather.2.cloned.1.call-start = ((), (), s32[]{:S(2)}) async-start(), calls=%async_computation.2 | async-start | bytes 2621440 | tf_op jit(solution)/shard_map/all_gather | solution.py:69
  16.2 45.6 %copy-start.6 = (f32[3,4,128]{2,1,0:T(4,128)}, f32[3,4,128]{2,1,0:T(4,128)S(1)}, u32[]{:S(2)}) copy-start(f32[3,4,128]{2,1,0:T(4,128)S(1)} %get-tuple-element.53) | copy-start | bytes 18436
  16.2 45.6 %copy-start.8 = (f32[3,4,128]{2,1,0:T(4,128)}, f32[3,4,128]{2,1,0:T(4,128)S(1)}, u32[]{:S(2)}) copy-start(f32[3,4,128]{2,1,0:T(4,128)S(1)} %get-tuple-element.54) | copy-start | bytes 18436
  16.2 45.6 %copy-start.10 = (f32[3,4,128]{2,1,0:T(4,128)}, f32[3,4,128]{2,1,0:T(4,128)S(1)}, u32[]{:S(2)}) copy-start(f32[3,4,128]{2,1,0:T(4,128)S(1)} %get-tuple-element.55) | copy-start | bytes 18436
  16.2 45.6 %copy-start.12 = (f32[3,4,128]{2,1,0:T(4,128)}, f32[3,4,128]{2,1,0:T(4,128)S(1)}, u32[]{:S(2)}) copy-start(f32[3,4,128]{2,1,0:T(4,128)S(1)} %get-tuple-element.56) | copy-start | bytes 18436
  16.2 45.6 %copy-start.14 = (f32[3,4,128]{2,1,0:T(4,128)}, f32[3,4,128]{2,1,0:T(4,128)S(1)}, u32[]{:S(2)}) copy-start(f32[3,4,128]{2,1,0:T(4,128)S(1)} %get-tuple-element.57) | copy-start | bytes 18436
  16.2 45.6 %copy-start.16 = (f32[3,4,128]{2,1,0:T(4,128)}, f32[3,4,128]{2,1,0:T(4,128)S(1)}, u32[]{:S(2)}) copy-start(f32[3,4,128]{2,1,0:T(4,128)S(1)} %get-tuple-element.58) | copy-start | bytes 18436
  16.2 45.6 %copy-start.18 = (f32[3,4,128]{2,1,0:T(4,128)}, f32[3,4,128]{2,1,0:T(4,128)S(1)}, u32[]{:S(2)}) copy-start(f32[3,4,128]{2,1,0:T(4,128)S(1)} %get-tuple-element.59) | copy-start | bytes 18436
  16.2 45.6 %copy-start.20 = (f32[3,4,128]{2,1,0:T(4,128)}, f32[3,4,128]{2,1,0:T(4,128)S(1)}, u32[]{:S(2)}) copy-start(f32[3,4,128]{2,1,0:T(4,128)S(1)} %get-tuple-element.60) | copy-start | bytes 18436
  16.2 45.6 %copy-start.22 = (f32[3,4,128]{2,1,0:T(4,128)}, f32[3,4,128]{2,1,0:T(4,128)S(1)}, u32[]{:S(2)}) copy-start(f32[3,4,128]{2,1,0:T(4,128)S(1)} %get-tuple-element.61) | copy-start | bytes 18436
  16.2 45.6 %copy-start.24 = (f32[3,4,128]{2,1,0:T(4,128)}, f32[3,4,128]{2,1,0:T(4,128)S(1)}, u32[]{:S(2)}) copy-start(f32[3,4,128]{2,1,0:T(4,128)S(1)} %get-tuple-element.62) | copy-start | bytes 18436
  16.3 45.6 %copy-start.26 = (f32[3,4,128]{2,1,0:T(4,128)}, f32[3,4,128]{2,1,0:T(4,128)S(1)}, u32[]{:S(2)}) copy-start(f32[3,4,128]{2,1,0:T(4,128)S(1)} %get-tuple-element.63) | copy-start | bytes 18436
  16.3 45.6 %copy-start.28 = (f32[3,4,128]{2,1,0:T(4,128)}, f32[3,4,128]{2,1,0:T(4,128)S(1)}, u32[]{:S(2)}) copy-start(f32[3,4,128]{2,1,0:T(4,128)S(1)} %get-tuple-element.64) | copy-start | bytes 18436
  16.3 45.6 %copy-start.30 = (f32[3,4,128]{2,1,0:T(4,128)}, f32[3,4,128]{2,1,0:T(4,128)S(1)}, u32[]{:S(2)}) copy-start(f32[3,4,128]{2,1,0:T(4,128)S(1)} %get-tuple-element.65) | copy-start | bytes 18436
  40.0 6.6 %copy-start.2 = (bf16[512,2048]{1,0:T(8,128)(2,1)S(1)}, bf16[512,2048]{1,0:T(8,128)(2,1)}, u32[]{:S(2)}) copy-start(bf16[512,2048]{1,0:T(8,128)(2,1)} %param.9) | copy-start | bytes 6291460
  40.1 21.6 %copy-start = (bf16[128,3,4,4,128]{4,0,2,3,1:T(8,128)(2,1)}, bf16[128,3,4,4,128]{4,0,2,3,1:T(8,128)(2,1)S(1)}, u32[]{:S(2)}) copy-start(bf16[128,3,4,4,128]{4,0,2,3,1:T(8,128)(2,1)S(1)} %copy.49) | copy-start | bytes 4718596
  40.2 20.6 %collective-permute-start = (bf16[256,3,4,128]{3,0,2,1:T(8,128)(2,1)S(1)}, bf16[256,3,4,128]{3,0,2,1:T(8,128)(2,1)S(1)}, u32[]{:S(2)}, u32[]{:S(2)}) collective-permute-start(bf16[256,3,4,128]{3,0,2,1:T(8,128)(2,1)S(1)} %bitcast.129), channel_id=1, source_target_pairs={{0,4},{4,8},{8,12},{12,16},{16,20},{20,24},{24,28},{1,5},{5,9},{9,... | collective-permute-start | bytes 2359304 | tf_op jit(solution)/shard_map/ppermute | solution.py:14
  91.6 3.7 %copy-start.1 = (bf16[768,3,4,128]{3,0,2,1:T(8,128)(2,1)S(1)}, bf16[768,3,4,128]{3,0,2,1:T(8,128)(2,1)}, u32[]{:S(2)}) copy-start(bf16[768,3,4,128]{3,0,2,1:T(8,128)(2,1)} %add_convert_fusion) | copy-start | bytes 7077892
  95.3 3.3 %copy-start.4 = (bf16[512,512]{1,0:T(8,128)(2,1)}, bf16[512,512]{1,0:T(8,128)(2,1)S(1)}, u32[]{:S(2)}) copy-start(bf16[512,512]{1,0:T(8,128)(2,1)S(1)} %convolution_convert_fusion) | copy-start | bytes 1572868
  137.2 4.2 %copy-start.3 = (f32[640,4,128]{2,0,1:T(8,128)S(1)}, f32[640,4,128]{2,0,1:T(8,128)}, u32[]{:S(2)}) copy-start(f32[640,4,128]{2,0,1:T(8,128)} %fusion.30) | copy-start | bytes 3932164
  141.8 0.7 copy-start.21
  141.8 0.7 copy-start.23
  141.8 0.7 copy-start.25
  141.8 0.8 copy-start.27
  141.8 0.8 copy-start.29
  141.8 0.8 copy-start.31
  161.4 20.0 %collective-permute-start.1 = (bf16[256,3,4,128]{3,0,2,1:T(8,128)(2,1)S(1)}, bf16[256,3,4,128]{3,0,2,1:T(8,128)(2,1)S(1)}, u32[]{:S(2)}, u32[]{:S(2)}) collective-permute-start(bf16[256,3,4,128]{3,0,2,1:T(8,128)(2,1)S(1)} %get-tuple-element.30), channel_id=1, source_target_pairs={{4,0},{8,4},{12,8},{16,12},{20,16},{24,20},{28,24},{5,1},{9,5},{13... | collective-permute-start | bytes 2359304 | tf_op jit(solution)/shard_map/ppermute | solution.py:14
  (7 other events, 5.0 us)
Sparse Core Ops, SparseCore 0:
  16.3 30.4 all-gather.1
where the time goes:
time: 215 us; the launch traced here: 214 us
  matrix products  62.2 us (29%)
  waiting for transfers between devices  52.9 us (25%)
  other arithmetic  43.8 us (20%)
  blocking collectives  22.7 us (11%)
  between operations  14 us (7%)
  starting transfers between devices  10.6 us (5%)
  local copies, waits for them, and re-layouts  7.9 us (4%)
    ppermute x2, waiting for transfers between devices, shifted(): return lax.ppermute(value, axis, pairs)  29.6 us
    all_to_all x1, blocking collectives, per_device(): lax.all_to_all(result, 'head', split_axis=0, concat_axis=2, tiled=True)  22.7 us
    all_to_all x1, waiting for transfers between devices, per_device(): lax.all_to_all(qkv_pre, 'head', split_axis=2, concat_axis=0, tiled=True)  22.6 us
    dot_general x1, matrix products, attend(): jnp.einsum('hqk,qhe->khe', d_score, q_block, preferred_element_type=jnp.f...  20.8 us
    convert_element_type x1, other arithmetic, per_device(): mixed_rows = causal_conv(extended, conv_kernel).astype(jnp.bfloat16)  20.5 us
    another operation x2, other arithmetic  18.9 us
    dot_general x1, matrix products, attend(): jnp.einsum('hqk,khe->qhe', d_score, k_block, preferred_element_type=jnp.f...  17.9 us
    sub x1, matrix products, attend(): exp_scores = jnp.where(allowed, jnp.exp(scores - row_top), 0.0)  9.22 us
  transfers between devices with their start and end apart: 4, of which 3 were waited for; matrix products, arithmetic and copies ran while one was open for 18% of the time, Pallas kernels for 0%

commit v1 on v0

--- a/solution.py
+++ b/solution.py
@@ -72,7 +72,15 @@
         preferred_element_type=jnp.float32,
     ).astype(jnp.bfloat16)
     grad_heads = grad_heads.reshape(seq_rows, local_heads, head_dim)
-    mixed_in = lax.all_to_all(qkv_pre, "head", split_axis=2, concat_axis=0, tiled=True)
+    ways, here = (lax.axis_size("head"), lax.axis_index("head"))
+    width = qkv_pre.shape[2] // ways
+    turned = jnp.roll(qkv_pre, -here * width, axis=2)
+    got = [lax.slice_in_dim(turned, 0, width, axis=2)]
+    for far in range(1, ways):
+        sent = lax.slice_in_dim(turned, far * width, (far + 1) * width, axis=2)
+        got.append(lax.ppermute(sent, "head", [(d, (d + far) % ways) for d in range(ways)]))
+    line = jnp.concatenate(got[::-1], axis=0)
+    mixed_in = jnp.roll(line, (here + 1) * got[0].shape[0], axis=0)
     tail_rows = mixed_in[seq_rows - prior :]
     before = shifted(tail_rows, "seq", 1)
     extended = jnp.concatenate([before, mixed_in], axis=0)

time: 215 us -> 214 us (level)
  local copies, waits for them, and re-layouts: 7.9 us -> 12.2 us
  waiting for transfers between devices: 52.9 us -> 49 us
  starting transfers between devices: 10.6 us -> 7.78 us
    all_to_all x1 -> x0, waiting for transfers between devices: 22.6 us -> none  [per_device(): lax.all_to_all(qkv_pre, 'head', split_axis=2, concat_axis=0, tiled=True)]
    ppermute x0 -> x3, waiting for transfers between devices: none -> 19.6 us  [per_device(): lax.ppermute(sent, 'head', [(d, (d + far) % ways) for d in range(ways)])]
    all_to_all x1 -> x0, starting transfers between devices: 4.37 us -> none  [per_device(): lax.all_to_all(qkv_pre, 'head', split_axis=2, concat_axis=0, tiled=True)]
    ppermute x0 -> x3, starting transfers between devices: none -> 3.2 us  [per_device(): lax.ppermute(sent, 'head', [(d, (d + far) % ways) for d in range(ways)])]
  transfers between devices with their start and end apart: 4 -> 6, of which waited for: 3 -> 4; matrix products, arithmetic and copies ran while one was open for 18% -> 20% of each run, Pallas kernels for 0% -> 0%
where the time goes in v1:
time: 214 us; the launch traced here: 213 us
  matrix products  62.4 us (29%)
  waiting for transfers between devices  49 us (23%)
  other arithmetic  45 us (21%)
  blocking collectives  22.5 us (11%)
  between operations  14.3 us (7%)
  local copies, waits for them, and re-layouts  12.2 us (6%)
  starting transfers between devices  7.78 us (4%)
    ppermute x2, waiting for transfers between devices, shifted(): return lax.ppermute(value, axis, pairs)  29.3 us
    all_to_all x1, blocking collectives, per_device(): lax.all_to_all(result, 'head', split_axis=0, concat_axis=2, tiled=True)  22.5 us
    dot_general x1, matrix products, attend(): jnp.einsum('hqk,qhe->khe', d_score, q_block, preferred_element_type=jnp.f...  20.9 us
    convert_element_type x1, other arithmetic, per_device(): mixed_rows = causal_conv(extended, conv_kernel).astype(jnp.bfloat16)  20.5 us
    ppermute x3, waiting for transfers between devices, per_device(): lax.ppermute(sent, 'head', [(d, (d + far) % ways) for d in range(ways)])  19.6 us
    another operation x2, other arithmetic  18.9 us
    dot_general x1, matrix products, attend(): jnp.einsum('hqk,khe->qhe', d_score, k_block, preferred_element_type=jnp.f...  18 us
    sub x1, matrix products, attend(): exp_scores = jnp.where(allowed, jnp.exp(scores - row_top), 0.0)  9.09 us
  transfers between devices with their start and end apart: 6, of which 4 were waited for; matrix products, arithmetic and copies ran while one was open for 20% of the time, Pallas kernels for 0%

profile of v1, /device:TPU:0, one launch (start us, length us, event | category | flops | bytes accessed | tf_op | source)
XLA Modules:
  0.0 213.1 jit_solution(12444466828085359153)
XLA Ops:
  6.5 1.8 copy.17
  8.4 0.6 fusion.26
  9.0 0.9 fusion.55
  9.8 2.4 %collective-permute-start = (bf16[128,3,4,128]{3,0,2,1:T(8,128)(2,1)}, bf16[128,3,4,128]{3,0,2,1:T(8,128)(2,1)S(1)}, u32[]{:S(2)}, u32[]{:S(2)}) collective-permute-start(bf16[128,3,4,128]{3,0,2,1:T(8,128)(2,1)} %get-tuple-element.33), channel_id=1, source_target_pairs={{0,3},{1,0},{2,1},{3,2},{4,7},{5,4},{6,5},{7,6},{8,11},{9,8},{10,9... | collective-permute-start | bytes 1179656 | tf_op jit(solution)/shard_map/ppermute | solution.py:81
  12.2 0.6 collective-permute-start.1
  13.1 1.1 compare_and_fusion.2
  14.2 1.5 slice_bitcast_fusion.46
  15.7 1.5 slice_bitcast_fusion.45
  17.3 1.4 dynamic_slice.41
  18.7 3.4 %collective-permute-done = bf16[128,3,4,128]{3,0,2,1:T(8,128)(2,1)S(1)} collective-permute-done((bf16[128,3,4,128]{3,0,2,1:T(8,128)(2,1)}, bf16[128,3,4,128]{3,0,2,1:T(8,128)(2,1)S(1)}, u32[]{:S(2)}, u32[]{:S(2)}) %collective-permute-start) | collective-permute-done | bytes 393248 | tf_op jit(solution)/shard_map/ppermute | solution.py:81
  22.1 16.3 %collective-permute-done.1 = bf16[128,3,4,128]{3,0,2,1:T(8,128)(2,1)S(1)} collective-permute-done((bf16[128,3,4,128]{3,0,2,1:T(8,128)(2,1)S(1)}, bf16[128,3,4,128]{3,0,2,1:T(8,128)(2,1)S(1)}, u32[]{:S(2)}, u32[]{:S(2)}) %collective-permute-start.1) | collective-permute-done | bytes 393248 | tf_op jit(solution)/shard_map/ppermute | solution.py:81
  39.0 3.3 %collective-permute-start.3 = (bf16[256,3,4,128]{3,0,2,1:T(8,128)(2,1)S(1)}, bf16[256,3,4,128]{3,0,2,1:T(8,128)(2,1)S(1)}, u32[]{:S(2)}, u32[]{:S(2)}) collective-permute-start(bf16[256,3,4,128]{3,0,2,1:T(8,128)(2,1)S(1)} %constant_dynamic-slice_fusion.1), channel_id=1, source_target_pairs={{0,4},{4,8},{8,12},{12,16},{16,20},{20,24},{24,28},{1,5},{5,9},{9,... | collective-permute-start | bytes 2359304 | tf_op jit(solution)/shard_map/ppermute | solution.py:14
  42.3 1.3 dynamic-slice_add_fusion
  43.6 1.3 broadcast_subtract_fusion
  45.0 3.4 %multiply_convert_fusion.1 = bf16[512,2048]{1,0:T(8,128)(2,1)} fusion(bf16[512,2048]{1,0:T(8,128)(2,1)S(1)} %copy-done.2, f32[2,8,16,128]{3,2,1,0:T(8,128)S(1)} %bitcast.120, s32[512]{0:T(512)S(1)} %add_select_fusion), kind=kOutput, calls=%fused_computation.16 | convolution fusion | flops 204480512 | bytes 4327424 | tf_op jit(solution)/shard_map/dot_general | solution.py:48
  48.6 0.4 constant_dynamic-slice_fusion
  49.1 9.8 %collective-permute-done.3 = bf16[256,3,4,128]{3,0,2,1:T(8,128)(2,1)S(1)} collective-permute-done((bf16[256,3,4,128]{3,0,2,1:T(8,128)(2,1)S(1)}, bf16[256,3,4,128]{3,0,2,1:T(8,128)(2,1)S(1)}, u32[]{:S(2)}, u32[]{:S(2)}) %collective-permute-start.3) | collective-permute-done | bytes 786464 | tf_op jit(solution)/shard_map/ppermute | solution.py:14
  58.9 0.9 pad_maximum_fusion.1
  60.1 20.5 %add_convert_fusion = bf16[768,3,4,128]{3,0,2,1:T(8,128)(2,1)} fusion(bf16[798,3,4,128]{3,0,2,1:T(8,128)(2,1)S(1)} %pad_maximum_fusion.1, bf16[512,3,4,128]{3,0,2,1:T(8,128)(2,1)} %copy-done, bf16[256,3,4,128]{3,0,2,1:T(8,128)(2,1)S(1)} %collective-permute-done.3, f32[3,4,128]{2,1,0:T(4,128)S(1)} %copy-done.13, f32[3,4,128]{2,1,0:T(4,128)S(1)} %copy-done.14, ...), kind=kLoop, calls=%fused_computation.15 | loop fusion | flops 113246208 | bytes 75687936 | tf_op jit(solution)/shard_map/convert_element_type | solution.py:87
  80.6 9.1 %fusion.56 = (f32[4,512]{1,0:T(4,128)}, f32[4,512,640]{2,1,0:T(8,128)}) fusion(s32[512,640]{1,0:T(8,128)} %broadcast_subtract_fusion, s32[4]{0:T(128)S(1)} %dynamic-slice_add_fusion, pred[512,640]{1,0:T(8,128)(4,1)} %compare_and_fusion.2, bf16[768,3,4,128]{3,0,2,1:T(8,128)(2,1)} %add_convert_fusion), kind=kOutput, calls=%fused_computation.118 | convolution fusion | flops 684196480 | bytes 10888192 | tf_op jit(solution)/shard_map/while/body/eval_jaxpr/sub | solution.py:117
  89.7 3.7 %convolution_convert_fusion = bf16[512,512]{1,0:T(8,128)(2,1)S(1)} fusion(bf16[512,2048]{1,0:T(8,128)(2,1)} %multiply_convert_fusion.1, bf16[512,2048]{1,0:T(8,128)(2,1)} %all-gather.2.cloned.1.call-done), kind=kOutput, calls=%fused_computation.43 | convolution fusion | flops 1074003968 | bytes 4718592 | tf_op jit(solution)/shard_map/dot_general | solution.py:68
  93.4 3.3 %fusion.39 = f32[4,512,640]{2,1,0:T(8,128)} fusion(bf16[512,4,128]{0,2,1:T(8,128)(2,1)S(1)} %bitcast.118, bf16[768,3,4,128]{3,0,2,1:T(8,128)(2,1)S(1)} %copy-done.1), kind=kOutput, calls=%fused_computation.46 | convolution fusion | flops 335544320 | bytes 6422528 | tf_op jit(solution)/shard_map/while/body/eval_jaxpr/qhe,khe->hqk/dot_general | solution.py:120
  96.6 18.0 %fusion.34 = f32[512,4,128]{2,0,1:T(8,128)S(1)} fusion(f32[4,512,640]{2,1,0:T(8,128)} %fusion.39, bf16[768,3,4,128]{3,0,2,1:T(8,128)(2,1)S(1)} %copy-done.1, f32[4,512,640]{2,1,0:T(8,128)} %get-tuple-element.80, f32[4,512]{1,0:T(4,128)} %get-tuple-element.79), kind=kOutput, calls=%fused_computation.41 | convolution fusion | flops 344722048 | bytes 22691840 | tf_op jit(solution)/shard_map/while/body/eval_jaxpr/hqk,khe->qhe/dot_general | solution.py:123
  114.6 20.9 %fusion.31 = f32[640,4,128]{2,0,1:T(8,128)} fusion(f32[4,512,640]{2,1,0:T(8,128)} %fusion.39, bf16[768,3,4,128]{3,0,2,1:T(8,128)(2,1)S(1)} %copy-done.1, f32[4,512,640]{2,1,0:T(8,128)} %get-tuple-element.80, f32[4,512]{1,0:T(4,128)} %get-tuple-element.79), kind=kOutput, calls=%fused_computation.40 | convolution fusion | flops 344722048 | bytes 22822912 | tf_op jit(solution)/shard_map/while/body/eval_jaxpr/hqk,qhe->khe/dot_general | solution.py:126
  135.5 4.1 %fusion.28 = f32[640,4,128]{2,0,1:T(8,128)S(1)} fusion(bf16[512,4,128]{0,2,1:T(8,128)(2,1)} %bitcast.119, f32[4,512,640]{2,1,0:T(8,128)} %get-tuple-element.80, f32[4,512]{1,0:T(4,128)} %get-tuple-element.79), kind=kOutput, calls=%fused_computation.39 | convolution fusion | flops 338165760 | bytes 7086080 | tf_op jit(solution)/shard_map/while/body/eval_jaxpr/hqk,qhe->khe/dot_general | solution.py:129
  140.1 0.3 pad_maximum_fusion
  140.9 18.6 %fusion.53 = (bf16[768,3,4,128]{3,0,2,1:T(8,128)(2,1)S(1)}, f32[768,3,4,128]{3,0,2,1:T(8,128)S(1)}) fusion(f32[3,4,128]{2,1,0:T(4,128)S(1)} %copy-done.13, f32[3,4,128]{2,1,0:T(4,128)S(1)} %copy-done.14, f32[3,4,128]{2,1,0:T(4,128)S(1)} %copy-done.16, f32[3,4,128]{2,1,0:T(4,128)S(1)} %copy-done.17, f32[3,4,128]{2,1,0:T(4,128)S(1)} %copy-done.18, ...), kind=kLoop, calls=%fused_computation.115 | loop fusion | flops 73138176 | bytes 11986944 | tf_op jit(solution)/shard_map/convert.2
  159.7 1.3 collective-permute-start.4
  161.0 19.5 %collective-permute-done.4 = bf16[256,3,4,128]{3,0,2,1:T(8,128)(2,1)S(1)} collective-permute-done((bf16[256,3,4,128]{3,0,2,1:T(8,128)(2,1)S(1)}, bf16[256,3,4,128]{3,0,2,1:T(8,128)(2,1)S(1)}, u32[]{:S(2)}, u32[]{:S(2)}) %collective-permute-start.4) | collective-permute-done | bytes 786464 | tf_op jit(solution)/shard_map/ppermute | solution.py:14
  180.9 1.2 copy.25
  182.1 22.5 %all_to_all.18 = bf16[512,3,4,128]{3,2,1,0:T(4,128)(2,1)S(1)} all-to-all(bf16[512,3,4,128]{3,2,1,0:T(4,128)(2,1)S(1)} %copy.25), channel_id=1, replica_groups=mesh['seq'=8,'head'=4] {'head'}, dimensions={0} | all-to-all | bytes 3145728 | tf_op jit(solution)/shard_map/all_to_all | solution.py:156
  204.6 1.7 copy.26
  (130 shorter events, 2.4 us)
Async XLA Ops:
  6.5 83.1 %all-gather.2.cloned.1.call-start = ((), (), s32[]{:S(2)}) async-start(), calls=%async_computation.1 | async-start | bytes 2621440 | tf_op jit(solution)/shard_map/all_gather | solution.py:69
  9.8 12.2 %collective-permute-start = (bf16[128,3,4,128]{3,0,2,1:T(8,128)(2,1)}, bf16[128,3,4,128]{3,0,2,1:T(8,128)(2,1)S(1)}, u32[]{:S(2)}, u32[]{:S(2)}) collective-permute-start(bf16[128,3,4,128]{3,0,2,1:T(8,128)(2,1)} %get-tuple-element.33), channel_id=1, source_target_pairs={{0,3},{1,0},{2,1},{3,2},{4,7},{5,4},{6,5},{7,6},{8,11},{9,8},{10,9... | collective-permute-start | bytes 1179656 | tf_op jit(solution)/shard_map/ppermute | solution.py:81
  12.2 26.1 %collective-permute-start.1 = (bf16[128,3,4,128]{3,0,2,1:T(8,128)(2,1)S(1)}, bf16[128,3,4,128]{3,0,2,1:T(8,128)(2,1)S(1)}, u32[]{:S(2)}, u32[]{:S(2)}) collective-permute-start(bf16[128,3,4,128]{3,0,2,1:T(8,128)(2,1)S(1)} %get-tuple-element.32), channel_id=1, source_target_pairs={{0,2},{1,3},{2,0},{3,1},{4,6},{5,7},{6,4},{7,5},{8,10},{9,11},{10,... | collective-permute-start | bytes 1179656 | tf_op jit(solution)/shard_map/ppermute | solution.py:81
  12.8 25.6 %collective-permute-start.2 = (bf16[128,3,4,128]{3,0,2,1:T(8,128)(2,1)S(1)}, bf16[128,3,4,128]{3,0,2,1:T(8,128)(2,1)S(1)}, u32[]{:S(2)}, u32[]{:S(2)}) collective-permute-start(bf16[128,3,4,128]{3,0,2,1:T(8,128)(2,1)S(1)} %get-tuple-element.31), channel_id=1, source_target_pairs={{0,1},{1,2},{2,3},{3,0},{4,5},{5,6},{6,7},{7,4},{8,9},{9,10},{10,1... | collective-permute-start | bytes 1179656 | tf_op jit(solution)/shard_map/ppermute | solution.py:81
  17.3 26.4 %copy-start.48 = (s32[640]{0:T(1024)S(1)}, s32[640]{0:T(1024)}, u32[]{:S(2)}) copy-start(s32[640]{0:T(1024)} %copy-done.47) | copy-start | bytes 7684
  17.3 26.4 %copy-start.50 = (s32[512]{0:T(512)S(1)}, s32[512]{0:T(512)}, u32[]{:S(2)}) copy-start(s32[512]{0:T(512)} %copy-done.49) | copy-start | bytes 6148
  17.3 27.6 %copy-start.51 = (f32[16,16]{1,0:T(8,128)S(1)}, f32[16,16]{1,0:T(8,128)}, u32[]{:S(2)}) copy-start(f32[16,16]{1,0:T(8,128)} %param.10) | copy-start | bytes 3076
  17.3 27.7 %copy-start.2 = (bf16[512,2048]{1,0:T(8,128)(2,1)S(1)}, bf16[512,2048]{1,0:T(8,128)(2,1)}, u32[]{:S(2)}) copy-start(bf16[512,2048]{1,0:T(8,128)(2,1)} %param.9) | copy-start | bytes 6291460
  39.0 19.9 %collective-permute-start.3 = (bf16[256,3,4,128]{3,0,2,1:T(8,128)(2,1)S(1)}, bf16[256,3,4,128]{3,0,2,1:T(8,128)(2,1)S(1)}, u32[]{:S(2)}, u32[]{:S(2)}) collective-permute-start(bf16[256,3,4,128]{3,0,2,1:T(8,128)(2,1)S(1)} %constant_dynamic-slice_fusion.1), channel_id=1, source_target_pairs={{0,4},{4,8},{8,12},{12,16},{16,20},{20,24},{24,28},{1,5},{5,9},{9,... | collective-permute-start | bytes 2359304 | tf_op jit(solution)/shard_map/ppermute | solution.py:14
  48.4 11.4 %copy-start.9 = (f32[3,4,128]{2,1,0:T(4,128)S(1)}, f32[3,4,128]{2,1,0:T(4,128)}, u32[]{:S(2)}) copy-start(f32[3,4,128]{2,1,0:T(4,128)} %get-tuple-element.73) | copy-start | bytes 18436
  48.4 11.4 %copy-start.10 = (f32[3,4,128]{2,1,0:T(4,128)S(1)}, f32[3,4,128]{2,1,0:T(4,128)}, u32[]{:S(2)}) copy-start(f32[3,4,128]{2,1,0:T(4,128)} %get-tuple-element.74) | copy-start | bytes 18436
  48.4 11.4 %copy-start.11 = (f32[3,4,128]{2,1,0:T(4,128)S(1)}, f32[3,4,128]{2,1,0:T(4,128)}, u32[]{:S(2)}) copy-start(f32[3,4,128]{2,1,0:T(4,128)} %get-tuple-element.75) | copy-start | bytes 18436
  48.4 11.4 %copy-start.12 = (f32[3,4,128]{2,1,0:T(4,128)S(1)}, f32[3,4,128]{2,1,0:T(4,128)}, u32[]{:S(2)}) copy-start(f32[3,4,128]{2,1,0:T(4,128)} %get-tuple-element.76) | copy-start | bytes 18436
  48.4 11.4 %copy-start.13 = (f32[3,4,128]{2,1,0:T(4,128)S(1)}, f32[3,4,128]{2,1,0:T(4,128)}, u32[]{:S(2)}) copy-start(f32[3,4,128]{2,1,0:T(4,128)} %get-tuple-element.77) | copy-start | bytes 18436
  48.4 11.4 %copy-start.14 = (f32[3,4,128]{2,1,0:T(4,128)S(1)}, f32[3,4,128]{2,1,0:T(4,128)}, u32[]{:S(2)}) copy-start(f32[3,4,128]{2,1,0:T(4,128)} %get-tuple-element.78) | copy-start | bytes 18436
  48.4 11.4 %copy-start.15 = (f32[3,4,128]{2,1,0:T(4,128)S(1)}, f32[3,4,128]{2,1,0:T(4,128)}, u32[]{:S(2)}) copy-start(f32[3,4,128]{2,1,0:T(4,128)} %get-tuple-element.34) | copy-start | bytes 18436
  48.5 11.4 %copy-start.16 = (f32[3,4,128]{2,1,0:T(4,128)S(1)}, f32[3,4,128]{2,1,0:T(4,128)}, u32[]{:S(2)}) copy-start(f32[3,4,128]{2,1,0:T(4,128)} %get-tuple-element.35) | copy-start | bytes 18436
  48.5 11.4 %copy-start.17 = (f32[3,4,128]{2,1,0:T(4,128)S(1)}, f32[3,4,128]{2,1,0:T(4,128)}, u32[]{:S(2)}) copy-start(f32[3,4,128]{2,1,0:T(4,128)} %get-tuple-element.48) | copy-start | bytes 18436
  48.5 11.4 %copy-start.18 = (f32[3,4,128]{2,1,0:T(4,128)S(1)}, f32[3,4,128]{2,1,0:T(4,128)}, u32[]{:S(2)}) copy-start(f32[3,4,128]{2,1,0:T(4,128)} %get-tuple-element.50) | copy-start | bytes 18436
  48.5 11.4 %copy-start.19 = (f32[3,4,128]{2,1,0:T(4,128)S(1)}, f32[3,4,128]{2,1,0:T(4,128)}, u32[]{:S(2)}) copy-start(f32[3,4,128]{2,1,0:T(4,128)} %get-tuple-element.52) | copy-start | bytes 18436
  48.5 11.4 %copy-start.20 = (f32[3,4,128]{2,1,0:T(4,128)S(1)}, f32[3,4,128]{2,1,0:T(4,128)}, u32[]{:S(2)}) copy-start(f32[3,4,128]{2,1,0:T(4,128)} %get-tuple-element.53) | copy-start | bytes 18436
  48.5 11.4 %copy-start.21 = (f32[3,4,128]{2,1,0:T(4,128)S(1)}, f32[3,4,128]{2,1,0:T(4,128)}, u32[]{:S(2)}) copy-start(f32[3,4,128]{2,1,0:T(4,128)} %get-tuple-element.54) | copy-start | bytes 18436
  48.5 11.4 %copy-start.23 = (f32[3,4,128]{2,1,0:T(4,128)S(1)}, f32[3,4,128]{2,1,0:T(4,128)}, u32[]{:S(2)}) copy-start(f32[3,4,128]{2,1,0:T(4,128)} %get-tuple-element.55) | copy-start | bytes 18436
  48.5 11.4 %copy-start.25 = (f32[3,4,128]{2,1,0:T(4,128)S(1)}, f32[3,4,128]{2,1,0:T(4,128)}, u32[]{:S(2)}) copy-start(f32[3,4,128]{2,1,0:T(4,128)} %get-tuple-element.56) | copy-start | bytes 18436
  48.5 11.4 %copy-start.27 = (f32[3,4,128]{2,1,0:T(4,128)S(1)}, f32[3,4,128]{2,1,0:T(4,128)}, u32[]{:S(2)}) copy-start(f32[3,4,128]{2,1,0:T(4,128)} %get-tuple-element.57) | copy-start | bytes 18436
  48.5 11.4 %copy-start.29 = (f32[3,4,128]{2,1,0:T(4,128)S(1)}, f32[3,4,128]{2,1,0:T(4,128)}, u32[]{:S(2)}) copy-start(f32[3,4,128]{2,1,0:T(4,128)} %get-tuple-element.58) | copy-start | bytes 18436
  48.5 11.4 %copy-start.31 = (f32[3,4,128]{2,1,0:T(4,128)S(1)}, f32[3,4,128]{2,1,0:T(4,128)}, u32[]{:S(2)}) copy-start(f32[3,4,128]{2,1,0:T(4,128)} %get-tuple-element.59) | copy-start | bytes 18436
  48.6 11.4 %copy-start.33 = (f32[3,4,128]{2,1,0:T(4,128)S(1)}, f32[3,4,128]{2,1,0:T(4,128)}, u32[]{:S(2)}) copy-start(f32[3,4,128]{2,1,0:T(4,128)} %get-tuple-element.60) | copy-start | bytes 18436
  48.6 11.4 %copy-start.35 = (f32[3,4,128]{2,1,0:T(4,128)S(1)}, f32[3,4,128]{2,1,0:T(4,128)}, u32[]{:S(2)}) copy-start(f32[3,4,128]{2,1,0:T(4,128)} %get-tuple-element.61) | copy-start | bytes 18436
  48.6 11.4 %copy-start.37 = (f32[3,4,128]{2,1,0:T(4,128)S(1)}, f32[3,4,128]{2,1,0:T(4,128)}, u32[]{:S(2)}) copy-start(f32[3,4,128]{2,1,0:T(4,128)} %get-tuple-element.62) | copy-start | bytes 18436
  48.6 11.4 %copy-start.39 = (f32[3,4,128]{2,1,0:T(4,128)S(1)}, f32[3,4,128]{2,1,0:T(4,128)}, u32[]{:S(2)}) copy-start(f32[3,4,128]{2,1,0:T(4,128)} %get-tuple-element.63) | copy-start | bytes 18436
  159.7 20.8 %collective-permute-start.4 = (bf16[256,3,4,128]{3,0,2,1:T(8,128)(2,1)S(1)}, bf16[256,3,4,128]{3,0,2,1:T(8,128)(2,1)S(1)}, u32[]{:S(2)}, u32[]{:S(2)}) collective-permute-start(bf16[256,3,4,128]{3,0,2,1:T(8,128)(2,1)S(1)} %get-tuple-element.30), channel_id=1, source_target_pairs={{4,0},{8,4},{12,8},{16,12},{20,16},{24,20},{28,24},{5,1},{9,5},{13... | collective-permute-start | bytes 2359304 | tf_op jit(solution)/shard_map/ppermute | solution.py:14
  (26 other events, 112.7 us)
Sparse Core Ops, SparseCore 0:
  13.2 30.5 all-gather.1
